TPU v7x, 128 devices: a whole 4x4x4 slice. The times are simulated.
128 devices in a mesh: row: 16 (over z, y_lo, core), col: 8 (over x, y_hi).
Axes of the slice: x: 4, y: 4 (y_hi: 2, y_lo: 2; y = y_hi * 2 + y_lo), z: 4, core: 2. Of those that a mesh axis runs over, the one named last changes fastest.
Arguments:
- query_proj: float32 [2048, 80, 128], P('col', 'row'), may hold values from -6 to 6
- key_proj: float32 [2048, 80, 128], P('col', 'row'), may hold values from -6 to 6
- value_proj: float32 [2048, 80, 128], P('col', 'row'), may hold values from -6 to 6
- out_grad: float32 [2048, 80, 128], P('col', 'row'), may hold values from -12 to 12
- pair_bias: float32 [4, 2048, 2048], P(None, 'row', 'col'), may hold values from -6 to 6
- log_sum_exp: float32 [4, 80, 2048], P(None, 'row', 'col'), as said below
- correction: float32 [4, 80, 2048], P(None, 'row', 'col'), may hold values from -12 to 12
- pad_mask: int32 [2048], replicated, may hold values from 0 to 1, as said below
Outputs:
- grad_query: float32 [2048, 80, 128], P('col', 'row')
- grad_key: float32 [2048, 80, 128], P('col', 'row')
- grad_value: float32 [2048, 80, 128], P('col', 'row')
- grad_bias: float32 [4, 2048, 2048], P(None, 'row', 'col')
Inputs may be any that keep to these rules, and one draw needn't show every extreme that they name: `pad_mask`: token 0 is always a real residue, about one token in eight is padding. `log_sum_exp`: each entry lies between log(2048) + 1 and log(2048) + 3.5.
All inputs are finite; a program needn't handle non-finite values.
Results may differ from a plain program's by a relative error of at most 0.0003.
Values sent between devices are 32-bit elements; how exact they have to be, the bound alone decides.
A program may use at most 128 MiB of HBM per device.

v0:
```python
import math
import jax
import jax.numpy as jnp
from jax import lax
from jax.sharding import PartitionSpec as P


def shifted(x, axis, by):
    length = lax.axis_size(axis)
    return lax.ppermute(x, axis, [(i, (i + by) % length) for i in range(length)])


def tile_terms(
    query_proj,
    out_grad,
    log_sum_exp,
    correction,
    bias_all,
    pad_mask,
    key_tile,
    value_tile,
    source,
    head_count,
):
    highest = lax.Precision.HIGHEST
    query_rows, columns, channels = query_proj.shape
    key_rows = key_tile.shape[0]
    head_size = channels // head_count
    inv_root = 1.0 / math.sqrt(head_size)
    query_heads = query_proj.reshape(query_rows, columns, head_count, head_size)
    grad_heads = out_grad.reshape(query_rows, columns, head_count, head_size)
    key_heads = key_tile.reshape(key_rows, columns, head_count, head_size)
    value_heads = value_tile.reshape(key_rows, columns, head_count, head_size)
    first_row = source * key_rows
    bias_block = lax.dynamic_slice_in_dim(bias_all, first_row, key_rows, 1)
    alive_keys = lax.dynamic_slice_in_dim(pad_mask, first_row, key_rows, 0) == 1
    scores = jnp.einsum("ijhd,kjhd->hjik", query_heads, key_heads, precision=highest) * inv_root
    scores = scores + jnp.transpose(bias_block, (0, 2, 1))[:, None, :, :]
    softmax_w = jnp.where(
        alive_keys[None, None, None, :],
        jnp.exp(scores - log_sum_exp[:, :, :, None]),
        jnp.float32(0.0),
    )
    prob_grad = jnp.einsum("ijhd,kjhd->hjik", grad_heads, value_heads, precision=highest)
    score_grad = softmax_w * (prob_grad - correction[:, :, :, None])
    query_part = jnp.einsum("hjik,kjhd->ijhd", score_grad, key_heads, precision=highest) * inv_root
    key_part = jnp.einsum("hjik,ijhd->kjhd", score_grad, query_heads, precision=highest) * inv_root
    value_part = jnp.einsum("hjik,ijhd->kjhd", softmax_w, grad_heads, precision=highest)
    bias_part = jnp.transpose(jnp.sum(score_grad, axis=1), (0, 2, 1))
    return (
        query_part.reshape(query_rows, columns, channels),
        key_part.reshape(key_rows, columns, channels),
        value_part.reshape(key_rows, columns, channels),
        bias_part,
    )


def body(query_proj, key_proj, value_proj, out_grad, pair_bias, log_sum_exp, correction, pad_mask):
    head_count = pair_bias.shape[0]
    col_count = lax.axis_size("col")
    own_col = lax.axis_index("col")
    key_rows = key_proj.shape[0]
    bias_all = lax.all_gather(pair_bias, "row", axis=1, tiled=True)

    def run_tile(key_tile, value_tile, source):
        return tile_terms(
            query_proj,
            out_grad,
            log_sum_exp,
            correction,
            bias_all,
            pad_mask,
            key_tile,
            value_tile,
            source,
            head_count,
        )

    query_grad, key_first, value_first, bias_first = run_tile(key_proj, value_proj, own_col)
    bias_total = jnp.zeros((head_count, pad_mask.shape[0], query_proj.shape[0]), jnp.float32)
    bias_total = lax.dynamic_update_slice_in_dim(bias_total, bias_first, own_col * key_rows, 1)

    def advance(turn, loop_state):
        key_tile, value_tile, key_accum, value_accum, query_accum, bias_accum = loop_state
        key_tile, value_tile, key_accum, value_accum = shifted(
            (key_tile, value_tile, key_accum, value_accum), "col", 1
        )
        source = (own_col - turn) % col_count
        query_part, key_part, value_part, bias_part = run_tile(key_tile, value_tile, source)
        bias_accum = lax.dynamic_update_slice_in_dim(bias_accum, bias_part, source * key_rows, 1)
        return (
            key_tile,
            value_tile,
            key_accum + key_part,
            value_accum + value_part,
            query_accum + query_part,
            bias_accum,
        )

    loop_state = lax.fori_loop(
        1,
        col_count,
        advance,
        (key_proj, value_proj, key_first, value_first, query_grad, bias_total),
    )
    query_grad = loop_state[4]
    bias_total = loop_state[5]
    grad_key, grad_value = shifted((loop_state[2], loop_state[3]), "col", 1)
    grad_bias = lax.psum_scatter(bias_total, "row", scatter_dimension=1, tiled=True)
    return (query_grad, grad_key, grad_value, grad_bias)


def solution(mesh):
    return jax.shard_map(
        body,
        mesh=mesh,
        in_specs=(
            P("col", "row", None),
            P("col", "row", None),
            P("col", "row", None),
            P("col", "row", None),
            P(None, "row", "col"),
            P(None, "row", "col"),
            P(None, "row", "col"),
            P(),
        ),
        out_specs=(
            P("col", "row", None),
            P("col", "row", None),
            P("col", "row", None),
            P(None, "row", "col"),
        ),
        check_vma=False,
    )
```

profile of v0, /device:TPU:17, one launch (start us, length us, event | category | flops | bytes accessed | tf_op | source)
XLA Modules:
  0.0 842.3 jit_solution(18110686419295969596)
XLA Ops:
  16.7 56.3 %all-gather.2.cloned.1.call-done = f32[4,2048,256]{1,2,0:T(8,128)} async-done(((f32[4,128,256]{1,2,0:T(8,128)}), f32[4,2048,256]{1,2,0:T(8,128)}) %all-gather.2.cloned.1.call-update) | async-done | bytes 8388624 | tf_op jit(solution)/shard_map/all_gather | solution.py:63
  74.3 6.7 exponential_select_fusion.1
  85.1 5.6 fusion.33
  90.7 6.0 fusion.25
  105.3 594.4 %while.25 = (s32[]{:T(128)}, f32[256,5,128]{0,2,1:T(8,128)}, f32[256,5,128]{0,2,1:T(8,128)}, f32[256,5,128]{0,2,1:T(8,128)}, f32[256,5,128]{0,2,1:T(8,128)}, /*i...) while((s32[]{:T(128)}, f32[256,5,128]{0,2,1:T(8,128)}, ...), condition=%wide.region_3.4_spmd, body=%wide.region_1.3_spmd.sunk | while | flops 2526314752 | bytes 63350792 | solution.py:100
  131.7 8.0 collective-permute-done
  139.7 5.6 exponential_select_fusion.3
  145.3 36.5 %collective-permute-done.1 = f32[256,5,128]{0,2,1:T(8,128)S(1)} collective-permute-done((f32[256,5,128]{0,2,1:T(8,128)}, f32[256,5,128]{0,2,1:T(8,128)S(1)}, u32[]{:S(2)}, u32[]{:S(2)}) %collective-permute-start.1) | collective-permute-done | bytes 655392 | tf_op jit(solution)/shard_map/while/body/eval_jaxpr/ppermute | solution.py:10
  215.5 7.3 collective-permute-done
  222.8 5.6 exponential_select_fusion.3
  228.3 36.5 %collective-permute-done.1 = f32[256,5,128]{0,2,1:T(8,128)S(1)} collective-permute-done((f32[256,5,128]{0,2,1:T(8,128)}, f32[256,5,128]{0,2,1:T(8,128)S(1)}, u32[]{:S(2)}, u32[]{:S(2)}) %collective-permute-start.1) | collective-permute-done | bytes 655392 | tf_op jit(solution)/shard_map/while/body/eval_jaxpr/ppermute | solution.py:10
  298.2 8.6 %collective-permute-done = f32[256,5,128]{0,2,1:T(8,128)S(1)} collective-permute-done((f32[256,5,128]{0,2,1:T(8,128)}, f32[256,5,128]{0,2,1:T(8,128)S(1)}, u32[]{:S(2)}, u32[]{:S(2)}) %collective-permute-start) | collective-permute-done | bytes 655392 | tf_op jit(solution)/shard_map/while/body/eval_jaxpr/ppermute | solution.py:10
  306.9 5.6 exponential_select_fusion.3
  312.5 36.5 %collective-permute-done.1 = f32[256,5,128]{0,2,1:T(8,128)S(1)} collective-permute-done((f32[256,5,128]{0,2,1:T(8,128)}, f32[256,5,128]{0,2,1:T(8,128)S(1)}, u32[]{:S(2)}, u32[]{:S(2)}) %collective-permute-start.1) | collective-permute-done | bytes 655392 | tf_op jit(solution)/shard_map/while/body/eval_jaxpr/ppermute | solution.py:10
  380.3 9.7 %collective-permute-done = f32[256,5,128]{0,2,1:T(8,128)S(1)} collective-permute-done((f32[256,5,128]{0,2,1:T(8,128)}, f32[256,5,128]{0,2,1:T(8,128)S(1)}, u32[]{:S(2)}, u32[]{:S(2)}) %collective-permute-start) | collective-permute-done | bytes 655392 | tf_op jit(solution)/shard_map/while/body/eval_jaxpr/ppermute | solution.py:10
  390.0 5.6 exponential_select_fusion.3
  395.6 36.5 %collective-permute-done.1 = f32[256,5,128]{0,2,1:T(8,128)S(1)} collective-permute-done((f32[256,5,128]{0,2,1:T(8,128)}, f32[256,5,128]{0,2,1:T(8,128)S(1)}, u32[]{:S(2)}, u32[]{:S(2)}) %collective-permute-start.1) | collective-permute-done | bytes 655392 | tf_op jit(solution)/shard_map/while/body/eval_jaxpr/ppermute | solution.py:10
  432.1 5.4 fusion.60
  462.1 10.1 %collective-permute-done = f32[256,5,128]{0,2,1:T(8,128)S(1)} collective-permute-done((f32[256,5,128]{0,2,1:T(8,128)}, f32[256,5,128]{0,2,1:T(8,128)S(1)}, u32[]{:S(2)}, u32[]{:S(2)}) %collective-permute-start) | collective-permute-done | bytes 655392 | tf_op jit(solution)/shard_map/while/body/eval_jaxpr/ppermute | solution.py:10
  472.2 5.6 exponential_select_fusion.3
  477.8 36.5 %collective-permute-done.1 = f32[256,5,128]{0,2,1:T(8,128)S(1)} collective-permute-done((f32[256,5,128]{0,2,1:T(8,128)}, f32[256,5,128]{0,2,1:T(8,128)S(1)}, u32[]{:S(2)}, u32[]{:S(2)}) %collective-permute-start.1) | collective-permute-done | bytes 655392 | tf_op jit(solution)/shard_map/while/body/eval_jaxpr/ppermute | solution.py:10
  543.0 10.3 %collective-permute-done = f32[256,5,128]{0,2,1:T(8,128)S(1)} collective-permute-done((f32[256,5,128]{0,2,1:T(8,128)}, f32[256,5,128]{0,2,1:T(8,128)S(1)}, u32[]{:S(2)}, u32[]{:S(2)}) %collective-permute-start) | collective-permute-done | bytes 655392 | tf_op jit(solution)/shard_map/while/body/eval_jaxpr/ppermute | solution.py:10
  553.4 5.6 exponential_select_fusion.3
  559.0 36.5 %collective-permute-done.1 = f32[256,5,128]{0,2,1:T(8,128)S(1)} collective-permute-done((f32[256,5,128]{0,2,1:T(8,128)}, f32[256,5,128]{0,2,1:T(8,128)S(1)}, u32[]{:S(2)}, u32[]{:S(2)}) %collective-permute-start.1) | collective-permute-done | bytes 655392 | tf_op jit(solution)/shard_map/while/body/eval_jaxpr/ppermute | solution.py:10
  623.1 10.6 %collective-permute-done = f32[256,5,128]{0,2,1:T(8,128)S(1)} collective-permute-done((f32[256,5,128]{0,2,1:T(8,128)}, f32[256,5,128]{0,2,1:T(8,128)S(1)}, u32[]{:S(2)}, u32[]{:S(2)}) %collective-permute-start) | collective-permute-done | bytes 655392 | tf_op jit(solution)/shard_map/while/body/eval_jaxpr/ppermute | solution.py:10
  633.7 5.6 exponential_select_fusion.3
  639.3 36.5 %collective-permute-done.1 = f32[256,5,128]{0,2,1:T(8,128)S(1)} collective-permute-done((f32[256,5,128]{0,2,1:T(8,128)}, f32[256,5,128]{0,2,1:T(8,128)S(1)}, u32[]{:S(2)}, u32[]{:S(2)}) %collective-permute-start.1) | collective-permute-done | bytes 655392 | tf_op jit(solution)/shard_map/while/body/eval_jaxpr/ppermute | solution.py:10
  675.8 5.4 fusion.60
  699.6 8.7 %copy.97 = f32[4,2048,256]{2,1,0:T(8,128)} copy(f32[4,2048,256]{1,2,0:T(8,128)} %get-tuple-element.341) | data formatting | bytes 16777216 | tf_op jit(solution)/shard_map/while | solution.py:100
  712.2 10.7 %collective-permute-done.4 = f32[256,5,128]{2,0,1:T(8,128)S(1)} collective-permute-done((f32[256,5,128]{2,0,1:T(8,128)S(1)}, f32[256,5,128]{2,0,1:T(8,128)S(1)}, u32[]{:S(2)}, u32[]{:S(2)}) %collective-permute-start.4) | collective-permute-done | bytes 655392 | tf_op jit(solution)/shard_map/ppermute | solution.py:10
  722.9 26.7 %collective-permute-done.5 = f32[256,5,128]{2,0,1:T(8,128)S(1)} collective-permute-done((f32[256,5,128]{2,0,1:T(8,128)S(1)}, f32[256,5,128]{2,0,1:T(8,128)S(1)}, u32[]{:S(2)}, u32[]{:S(2)}) %collective-permute-start.5) | collective-permute-done | bytes 655392 | tf_op jit(solution)/shard_map/ppermute | solution.py:10
  749.6 83.8 %reduce-scatter.2.cloned.1.call-done = f32[4,128,256]{2,1,0:T(8,128)} async-done(((f32[4,2048,256]{2,1,0:T(8,128)}), f32[4,128,256]{2,1,0:T(8,128)}) %reduce-scatter.2.cloned.1.call-update) | async-done | bytes 524304 | tf_op jit(solution)/shard_map/reduce_scatter | solution.py:109
  (154 shorter events, 236.0 us)
Async XLA Ops:
  7.2 65.8 %all-gather.2.cloned.1.call-start = ((), (), s32[]{:S(2)}) async-start(), calls=%async_computation.1 | async-start | bytes 8912896 | tf_op jit(solution)/shard_map/all_gather | solution.py:63
  9.3 824.1 %reduce-scatter.2.cloned.1.call-start = ((), (), s32[]{:S(2)}) async-start(), calls=%async_computation.2 | async-start | bytes 8912896 | tf_op jit(solution)/shard_map/reduce_scatter | solution.py:109
  121.8 17.9 %collective-permute-start = (f32[256,5,128]{0,2,1:T(8,128)}, f32[256,5,128]{0,2,1:T(8,128)S(1)}, u32[]{:S(2)}, u32[]{:S(2)}) collective-permute-start(f32[256,5,128]{0,2,1:T(8,128)} %get-tuple-element.538), channel_id=1, source_target_pairs={{0,1},{1,2},{2,3},{3,4},{4,5},{5,6},{6,7},{7,0},{8,9},{9,10},{10,1... | collective-permute-start | bytes 1966088 | tf_op jit(solution)/shard_map/while/body/eval_jaxpr/ppermute | solution.py:10
  123.3 74.9 %collective-permute-start.3 = (f32[256,5,128]{0,2,1:T(8,128)}, f32[256,5,128]{0,2,1:T(8,128)}, u32[]{:S(2)}, u32[]{:S(2)}) collective-permute-start(f32[256,5,128]{0,2,1:T(8,128)} %get-tuple-element.541), channel_id=1, source_target_pairs={{0,1},{1,2},{2,3},{3,4},{4,5},{5,6},{6,7},{7,0},{8,9},{9,10},{10,1... | collective-permute-start | bytes 1966088 | tf_op jit(solution)/shard_map/while/body/eval_jaxpr/ppermute | solution.py:10
  125.7 77.8 %collective-permute-start.2 = (f32[256,5,128]{0,2,1:T(8,128)}, f32[256,5,128]{0,2,1:T(8,128)}, u32[]{:S(2)}, u32[]{:S(2)}) collective-permute-start(f32[256,5,128]{0,2,1:T(8,128)} %get-tuple-element.540), channel_id=1, source_target_pairs={{0,1},{1,2},{2,3},{3,4},{4,5},{5,6},{6,7},{7,0},{8,9},{9,10},{10,1... | collective-permute-start | bytes 1966088 | tf_op jit(solution)/shard_map/while/body/eval_jaxpr/ppermute | solution.py:10
  127.2 54.6 %collective-permute-start.1 = (f32[256,5,128]{0,2,1:T(8,128)}, f32[256,5,128]{0,2,1:T(8,128)S(1)}, u32[]{:S(2)}, u32[]{:S(2)}) collective-permute-start(f32[256,5,128]{0,2,1:T(8,128)} %get-tuple-element.539), channel_id=1, source_target_pairs={{0,1},{1,2},{2,3},{3,4},{4,5},{5,6},{6,7},{7,0},{8,9},{9,10},{10,1... | collective-permute-start | bytes 1966088 | tf_op jit(solution)/shard_map/while/body/eval_jaxpr/ppermute | solution.py:10
  205.5 17.2 %collective-permute-start = (f32[256,5,128]{0,2,1:T(8,128)}, f32[256,5,128]{0,2,1:T(8,128)S(1)}, u32[]{:S(2)}, u32[]{:S(2)}) collective-permute-start(f32[256,5,128]{0,2,1:T(8,128)} %get-tuple-element.538), channel_id=1, source_target_pairs={{0,1},{1,2},{2,3},{3,4},{4,5},{5,6},{6,7},{7,0},{8,9},{9,10},{10,1... | collective-permute-start | bytes 1966088 | tf_op jit(solution)/shard_map/while/body/eval_jaxpr/ppermute | solution.py:10
  207.9 73.5 %collective-permute-start.3 = (f32[256,5,128]{0,2,1:T(8,128)}, f32[256,5,128]{0,2,1:T(8,128)}, u32[]{:S(2)}, u32[]{:S(2)}) collective-permute-start(f32[256,5,128]{0,2,1:T(8,128)} %get-tuple-element.541), channel_id=1, source_target_pairs={{0,1},{1,2},{2,3},{3,4},{4,5},{5,6},{6,7},{7,0},{8,9},{9,10},{10,1... | collective-permute-start | bytes 1966088 | tf_op jit(solution)/shard_map/while/body/eval_jaxpr/ppermute | solution.py:10
  209.5 77.2 %collective-permute-start.2 = (f32[256,5,128]{0,2,1:T(8,128)}, f32[256,5,128]{0,2,1:T(8,128)}, u32[]{:S(2)}, u32[]{:S(2)}) collective-permute-start(f32[256,5,128]{0,2,1:T(8,128)} %get-tuple-element.540), channel_id=1, source_target_pairs={{0,1},{1,2},{2,3},{3,4},{4,5},{5,6},{6,7},{7,0},{8,9},{9,10},{10,1... | collective-permute-start | bytes 1966088 | tf_op jit(solution)/shard_map/while/body/eval_jaxpr/ppermute | solution.py:10
  211.8 53.1 %collective-permute-start.1 = (f32[256,5,128]{0,2,1:T(8,128)}, f32[256,5,128]{0,2,1:T(8,128)S(1)}, u32[]{:S(2)}, u32[]{:S(2)}) collective-permute-start(f32[256,5,128]{0,2,1:T(8,128)} %get-tuple-element.539), channel_id=1, source_target_pairs={{0,1},{1,2},{2,3},{3,4},{4,5},{5,6},{6,7},{7,0},{8,9},{9,10},{10,1... | collective-permute-start | bytes 1966088 | tf_op jit(solution)/shard_map/while/body/eval_jaxpr/ppermute | solution.py:10
  288.7 18.2 %collective-permute-start = (f32[256,5,128]{0,2,1:T(8,128)}, f32[256,5,128]{0,2,1:T(8,128)S(1)}, u32[]{:S(2)}, u32[]{:S(2)}) collective-permute-start(f32[256,5,128]{0,2,1:T(8,128)} %get-tuple-element.538), channel_id=1, source_target_pairs={{0,1},{1,2},{2,3},{3,4},{4,5},{5,6},{6,7},{7,0},{8,9},{9,10},{10,1... | collective-permute-start | bytes 1966088 | tf_op jit(solution)/shard_map/while/body/eval_jaxpr/ppermute | solution.py:10
  291.5 74.0 %collective-permute-start.3 = (f32[256,5,128]{0,2,1:T(8,128)}, f32[256,5,128]{0,2,1:T(8,128)}, u32[]{:S(2)}, u32[]{:S(2)}) collective-permute-start(f32[256,5,128]{0,2,1:T(8,128)} %get-tuple-element.541), channel_id=1, source_target_pairs={{0,1},{1,2},{2,3},{3,4},{4,5},{5,6},{6,7},{7,0},{8,9},{9,10},{10,1... | collective-permute-start | bytes 1966088 | tf_op jit(solution)/shard_map/while/body/eval_jaxpr/ppermute | solution.py:10
  292.2 78.6 %collective-permute-start.2 = (f32[256,5,128]{0,2,1:T(8,128)}, f32[256,5,128]{0,2,1:T(8,128)}, u32[]{:S(2)}, u32[]{:S(2)}) collective-permute-start(f32[256,5,128]{0,2,1:T(8,128)} %get-tuple-element.540), channel_id=1, source_target_pairs={{0,1},{1,2},{2,3},{3,4},{4,5},{5,6},{6,7},{7,0},{8,9},{9,10},{10,1... | collective-permute-start | bytes 1966088 | tf_op jit(solution)/shard_map/while/body/eval_jaxpr/ppermute | solution.py:10
  295.5 53.5 %collective-permute-start.1 = (f32[256,5,128]{0,2,1:T(8,128)}, f32[256,5,128]{0,2,1:T(8,128)S(1)}, u32[]{:S(2)}, u32[]{:S(2)}) collective-permute-start(f32[256,5,128]{0,2,1:T(8,128)} %get-tuple-element.539), channel_id=1, source_target_pairs={{0,1},{1,2},{2,3},{3,4},{4,5},{5,6},{6,7},{7,0},{8,9},{9,10},{10,1... | collective-permute-start | bytes 1966088 | tf_op jit(solution)/shard_map/while/body/eval_jaxpr/ppermute | solution.py:10
  372.8 17.2 %collective-permute-start = (f32[256,5,128]{0,2,1:T(8,128)}, f32[256,5,128]{0,2,1:T(8,128)S(1)}, u32[]{:S(2)}, u32[]{:S(2)}) collective-permute-start(f32[256,5,128]{0,2,1:T(8,128)} %get-tuple-element.538), channel_id=1, source_target_pairs={{0,1},{1,2},{2,3},{3,4},{4,5},{5,6},{6,7},{7,0},{8,9},{9,10},{10,1... | collective-permute-start | bytes 1966088 | tf_op jit(solution)/shard_map/while/body/eval_jaxpr/ppermute | solution.py:10
  374.3 74.3 %collective-permute-start.3 = (f32[256,5,128]{0,2,1:T(8,128)}, f32[256,5,128]{0,2,1:T(8,128)}, u32[]{:S(2)}, u32[]{:S(2)}) collective-permute-start(f32[256,5,128]{0,2,1:T(8,128)} %get-tuple-element.541), channel_id=1, source_target_pairs={{0,1},{1,2},{2,3},{3,4},{4,5},{5,6},{6,7},{7,0},{8,9},{9,10},{10,1... | collective-permute-start | bytes 1966088 | tf_op jit(solution)/shard_map/while/body/eval_jaxpr/ppermute | solution.py:10
  374.4 79.6 %collective-permute-start.2 = (f32[256,5,128]{0,2,1:T(8,128)}, f32[256,5,128]{0,2,1:T(8,128)}, u32[]{:S(2)}, u32[]{:S(2)}) collective-permute-start(f32[256,5,128]{0,2,1:T(8,128)} %get-tuple-element.540), channel_id=1, source_target_pairs={{0,1},{1,2},{2,3},{3,4},{4,5},{5,6},{6,7},{7,0},{8,9},{9,10},{10,1... | collective-permute-start | bytes 1966088 | tf_op jit(solution)/shard_map/while/body/eval_jaxpr/ppermute | solution.py:10
  378.2 53.9 %collective-permute-start.1 = (f32[256,5,128]{0,2,1:T(8,128)}, f32[256,5,128]{0,2,1:T(8,128)S(1)}, u32[]{:S(2)}, u32[]{:S(2)}) collective-permute-start(f32[256,5,128]{0,2,1:T(8,128)} %get-tuple-element.539), channel_id=1, source_target_pairs={{0,1},{1,2},{2,3},{3,4},{4,5},{5,6},{6,7},{7,0},{8,9},{9,10},{10,1... | collective-permute-start | bytes 1966088 | tf_op jit(solution)/shard_map/while/body/eval_jaxpr/ppermute | solution.py:10
  455.9 16.3 %collective-permute-start = (f32[256,5,128]{0,2,1:T(8,128)}, f32[256,5,128]{0,2,1:T(8,128)S(1)}, u32[]{:S(2)}, u32[]{:S(2)}) collective-permute-start(f32[256,5,128]{0,2,1:T(8,128)} %get-tuple-element.538), channel_id=1, source_target_pairs={{0,1},{1,2},{2,3},{3,4},{4,5},{5,6},{6,7},{7,0},{8,9},{9,10},{10,1... | collective-permute-start | bytes 1966088 | tf_op jit(solution)/shard_map/while/body/eval_jaxpr/ppermute | solution.py:10
  456.2 74.7 %collective-permute-start.3 = (f32[256,5,128]{0,2,1:T(8,128)}, f32[256,5,128]{0,2,1:T(8,128)}, u32[]{:S(2)}, u32[]{:S(2)}) collective-permute-start(f32[256,5,128]{0,2,1:T(8,128)} %get-tuple-element.541), channel_id=1, source_target_pairs={{0,1},{1,2},{2,3},{3,4},{4,5},{5,6},{6,7},{7,0},{8,9},{9,10},{10,1... | collective-permute-start | bytes 1966088 | tf_op jit(solution)/shard_map/while/body/eval_jaxpr/ppermute | solution.py:10
  456.2 79.9 %collective-permute-start.2 = (f32[256,5,128]{0,2,1:T(8,128)}, f32[256,5,128]{0,2,1:T(8,128)}, u32[]{:S(2)}, u32[]{:S(2)}) collective-permute-start(f32[256,5,128]{0,2,1:T(8,128)} %get-tuple-element.540), channel_id=1, source_target_pairs={{0,1},{1,2},{2,3},{3,4},{4,5},{5,6},{6,7},{7,0},{8,9},{9,10},{10,1... | collective-permute-start | bytes 1966088 | tf_op jit(solution)/shard_map/while/body/eval_jaxpr/ppermute | solution.py:10
  460.0 54.3 %collective-permute-start.1 = (f32[256,5,128]{0,2,1:T(8,128)}, f32[256,5,128]{0,2,1:T(8,128)S(1)}, u32[]{:S(2)}, u32[]{:S(2)}) collective-permute-start(f32[256,5,128]{0,2,1:T(8,128)} %get-tuple-element.539), channel_id=1, source_target_pairs={{0,1},{1,2},{2,3},{3,4},{4,5},{5,6},{6,7},{7,0},{8,9},{9,10},{10,1... | collective-permute-start | bytes 1966088 | tf_op jit(solution)/shard_map/while/body/eval_jaxpr/ppermute | solution.py:10
  538.2 15.2 %collective-permute-start = (f32[256,5,128]{0,2,1:T(8,128)}, f32[256,5,128]{0,2,1:T(8,128)S(1)}, u32[]{:S(2)}, u32[]{:S(2)}) collective-permute-start(f32[256,5,128]{0,2,1:T(8,128)} %get-tuple-element.538), channel_id=1, source_target_pairs={{0,1},{1,2},{2,3},{3,4},{4,5},{5,6},{6,7},{7,0},{8,9},{9,10},{10,1... | collective-permute-start | bytes 1966088 | tf_op jit(solution)/shard_map/while/body/eval_jaxpr/ppermute | solution.py:10
  538.2 73.8 %collective-permute-start.3 = (f32[256,5,128]{0,2,1:T(8,128)}, f32[256,5,128]{0,2,1:T(8,128)}, u32[]{:S(2)}, u32[]{:S(2)}) collective-permute-start(f32[256,5,128]{0,2,1:T(8,128)} %get-tuple-element.541), channel_id=1, source_target_pairs={{0,1},{1,2},{2,3},{3,4},{4,5},{5,6},{6,7},{7,0},{8,9},{9,10},{10,1... | collective-permute-start | bytes 1966088 | tf_op jit(solution)/shard_map/while/body/eval_jaxpr/ppermute | solution.py:10
  538.2 79.1 %collective-permute-start.2 = (f32[256,5,128]{0,2,1:T(8,128)}, f32[256,5,128]{0,2,1:T(8,128)}, u32[]{:S(2)}, u32[]{:S(2)}) collective-permute-start(f32[256,5,128]{0,2,1:T(8,128)} %get-tuple-element.540), channel_id=1, source_target_pairs={{0,1},{1,2},{2,3},{3,4},{4,5},{5,6},{6,7},{7,0},{8,9},{9,10},{10,1... | collective-permute-start | bytes 1966088 | tf_op jit(solution)/shard_map/while/body/eval_jaxpr/ppermute | solution.py:10
  540.9 54.6 %collective-permute-start.1 = (f32[256,5,128]{0,2,1:T(8,128)}, f32[256,5,128]{0,2,1:T(8,128)S(1)}, u32[]{:S(2)}, u32[]{:S(2)}) collective-permute-start(f32[256,5,128]{0,2,1:T(8,128)} %get-tuple-element.539), channel_id=1, source_target_pairs={{0,1},{1,2},{2,3},{3,4},{4,5},{5,6},{6,7},{7,0},{8,9},{9,10},{10,1... | collective-permute-start | bytes 1966088 | tf_op jit(solution)/shard_map/while/body/eval_jaxpr/ppermute | solution.py:10
  619.3 14.4 %collective-permute-start = (f32[256,5,128]{0,2,1:T(8,128)}, f32[256,5,128]{0,2,1:T(8,128)S(1)}, u32[]{:S(2)}, u32[]{:S(2)}) collective-permute-start(f32[256,5,128]{0,2,1:T(8,128)} %get-tuple-element.538), channel_id=1, source_target_pairs={{0,1},{1,2},{2,3},{3,4},{4,5},{5,6},{6,7},{7,0},{8,9},{9,10},{10,1... | collective-permute-start | bytes 1966088 | tf_op jit(solution)/shard_map/while/body/eval_jaxpr/ppermute | solution.py:10
  619.3 73.0 %collective-permute-start.3 = (f32[256,5,128]{0,2,1:T(8,128)}, f32[256,5,128]{0,2,1:T(8,128)}, u32[]{:S(2)}, u32[]{:S(2)}) collective-permute-start(f32[256,5,128]{0,2,1:T(8,128)} %get-tuple-element.541), channel_id=1, source_target_pairs={{0,1},{1,2},{2,3},{3,4},{4,5},{5,6},{6,7},{7,0},{8,9},{9,10},{10,1... | collective-permute-start | bytes 1966088 | tf_op jit(solution)/shard_map/while/body/eval_jaxpr/ppermute | solution.py:10
  619.3 78.3 %collective-permute-start.2 = (f32[256,5,128]{0,2,1:T(8,128)}, f32[256,5,128]{0,2,1:T(8,128)}, u32[]{:S(2)}, u32[]{:S(2)}) collective-permute-start(f32[256,5,128]{0,2,1:T(8,128)} %get-tuple-element.540), channel_id=1, source_target_pairs={{0,1},{1,2},{2,3},{3,4},{4,5},{5,6},{6,7},{7,0},{8,9},{9,10},{10,1... | collective-permute-start | bytes 1966088 | tf_op jit(solution)/shard_map/while/body/eval_jaxpr/ppermute | solution.py:10
  620.9 54.9 %collective-permute-start.1 = (f32[256,5,128]{0,2,1:T(8,128)}, f32[256,5,128]{0,2,1:T(8,128)S(1)}, u32[]{:S(2)}, u32[]{:S(2)}) collective-permute-start(f32[256,5,128]{0,2,1:T(8,128)} %get-tuple-element.539), channel_id=1, source_target_pairs={{0,1},{1,2},{2,3},{3,4},{4,5},{5,6},{6,7},{7,0},{8,9},{9,10},{10,1... | collective-permute-start | bytes 1966088 | tf_op jit(solution)/shard_map/while/body/eval_jaxpr/ppermute | solution.py:10
  709.7 13.2 %collective-permute-start.4 = (f32[256,5,128]{2,0,1:T(8,128)S(1)}, f32[256,5,128]{2,0,1:T(8,128)S(1)}, u32[]{:S(2)}, u32[]{:S(2)}) collective-permute-start(f32[256,5,128]{2,0,1:T(8,128)S(1)} %copy.95), channel_id=1, source_target_pairs={{0,1},{1,2},{2,3},{3,4},{4,5},{5,6},{6,7},{7,0},{8,9},{9,10},{10,1... | collective-permute-start | bytes 1966088 | tf_op jit(solution)/shard_map/ppermute | solution.py:10
  711.1 38.5 %collective-permute-start.5 = (f32[256,5,128]{2,0,1:T(8,128)S(1)}, f32[256,5,128]{2,0,1:T(8,128)S(1)}, u32[]{:S(2)}, u32[]{:S(2)}) collective-permute-start(f32[256,5,128]{2,0,1:T(8,128)S(1)} %copy.96), channel_id=1, source_target_pairs={{0,1},{1,2},{2,3},{3,4},{4,5},{5,6},{6,7},{7,0},{8,9},{9,10},{10,1... | collective-permute-start | bytes 1966088 | tf_op jit(solution)/shard_map/ppermute | solution.py:10
  (3 other events, 81.1 us)
Sparse Core Ops, SparseCore 0:
  10.2 62.7 all-gather.1
  708.5 124.8 reduce-scatter.1
where the time goes:
time: 853 us; the launch traced here: 842 us
  waiting for transfers between devices  498 us (58%)
  matrix products  183 us (21%)
  local copies, waits for them, and re-layouts  57 us (7%)
  starting transfers between devices  37.4 us (4%)
  other arithmetic  35.2 us (4%)
  loops' own time  17 us (2%)
  between operations  14.6 us (2%)
    ppermute x30, waiting for transfers between devices, shifted(): lax.ppermute(x, axis, [(i, (i + by) % length) for i in range(length)])  358 us
    reduce_scatter x1, waiting for transfers between devices, body(): lax.psum_scatter(bias_total, 'row', scatter_dimension=1, tiled=True)  83.8 us
    all_gather x1, waiting for transfers between devices, body(): bias_all = lax.all_gather(pair_bias, 'row', axis=1, tiled=True)  56.3 us
    dot_general x8, matrix products, tile_terms(): jnp.einsum('ijhd,kjhd->hjik', query_heads, key_heads, precision=highest)  45.8 us
    dot_general x8, matrix products, tile_terms(): jnp.einsum('ijhd,kjhd->hjik', grad_heads, value_heads, precision=highest)  43.2 us
    dot_general x8, matrix products, tile_terms(): jnp.einsum('hjik,kjhd->ijhd', score_grad, key_heads, precision=highest)  40.2 us
    ppermute x30, starting transfers between devices, shifted(): lax.ppermute(x, axis, [(i, (i + by) % length) for i in range(length)])  37.3 us
    dot_general x8, matrix products, tile_terms(): jnp.einsum('hjik,ijhd->kjhd', softmax_w, grad_heads, precision=highest)  27 us
  transfers between devices with their start and end apart: 32, of which 18 were waited for; matrix products, arithmetic and copies ran while one was open for 26% of the time, Pallas kernels for 0%

commit v1 on v0

--- a/solution.py
+++ b/solution.py
@@ -60,7 +60,9 @@
     col_count = lax.axis_size("col")
     own_col = lax.axis_index("col")
     key_rows = key_proj.shape[0]
-    bias_all = lax.all_gather(pair_bias, "row", axis=1, tiled=True)
+    bias_all = jnp.concatenate(
+        lax.all_to_all(jnp.stack([pair_bias] * lax.axis_size("row")), "row", 0, 0), axis=1
+    )
 
     def run_tile(key_tile, value_tile, source):
         return tile_terms(

time: 853 us -> 887 us (1.040)
  local copies, waits for them, and re-layouts: 57 us -> 83.3 us
  loops' own time: 17 us -> 0.86 us
  matrix products: 183 us -> 194 us
  waiting for transfers between devices: 498 us -> 508 us
  starting transfers between devices: 37.4 us -> 47 us
    all_to_all x0 -> x1, waiting for transfers between devices: none -> 90 us  [body(): lax.all_to_all(jnp.stack([pair_bias] * lax.axis_size('row')), 'row', 0, 0)]
    all_gather x1 -> x0, waiting for transfers between devices: 56.3 us -> none  [body(): bias_all = lax.all_gather(pair_bias, 'row', axis=1, tiled=True)]
    ppermute x30, waiting for transfers between devices: 358 us -> 327 us  [shifted(): lax.ppermute(x, axis, [(i, (i + by) % length) for i in range(length)])]
    dynamic_slice x0 -> x14, local copies, waits for them, and re-layouts: none -> 18.3 us  [tile_terms(): bias_block = lax.dynamic_slice_in_dim(bias_all, first_row, key_rows, 1)]
    another operation x1, loops' own time: 17 us -> 0.86 us  [body(): lax.fori_loop(1, col_count, advance, (key_proj, value_proj, key_first, va...]
    dot_general x8, matrix products: 45.8 us -> 54.9 us  [tile_terms(): jnp.einsum('ijhd,kjhd->hjik', query_heads, key_heads, precision=highest)]
    all_to_all x0 -> x1, local copies, waits for them, and re-layouts: none -> 8.89 us  [body(): lax.all_to_all(jnp.stack([pair_bias] * lax.axis_size('row')), 'row', 0, 0)]
    while x14 -> x70, local copies, waits for them, and re-layouts: 11.7 us -> 17.8 us
where the time goes in v1:
time: 887 us; the launch traced here: 883 us
  waiting for transfers between devices  508 us (57%)
  matrix products  194 us (22%)
  local copies, waits for them, and re-layouts  83.3 us (9%)
  starting transfers between devices  47 us (5%)
  other arithmetic  35 us (4%)
  between operations  14.4 us (2%)
    ppermute x30, waiting for transfers between devices, shifted(): lax.ppermute(x, axis, [(i, (i + by) % length) for i in range(length)])  327 us
    reduce_scatter x1, waiting for transfers between devices, body(): lax.psum_scatter(bias_total, 'row', scatter_dimension=1, tiled=True)  91.1 us
    all_to_all x1, waiting for transfers between devices, body(): lax.all_to_all(jnp.stack([pair_bias] * lax.axis_size('row')), 'row', 0, 0)  90 us
    dot_general x8, matrix products, tile_terms(): jnp.einsum('ijhd,kjhd->hjik', query_heads, key_heads, precision=highest)  54.9 us
    dot_general x8, matrix products, tile_terms(): jnp.einsum('ijhd,kjhd->hjik', grad_heads, value_heads, precision=highest)  44.5 us
    dot_general x8, matrix products, tile_terms(): jnp.einsum('hjik,kjhd->ijhd', score_grad, key_heads, precision=highest)  41 us
    ppermute x30, starting transfers between devices, shifted(): lax.ppermute(x, axis, [(i, (i + by) % length) for i in range(length)])  40.1 us
    dot_general x8, matrix products, tile_terms(): jnp.einsum('hjik,ijhd->kjhd', score_grad, query_heads, precision=highest)  27 us
  transfers between devices with their start and end apart: 32, of which 18 were waited for; matrix products, arithmetic and copies ran while one was open for 26% of the time, Pallas kernels for 0%

profile of v1, /device:TPU:17, one launch (start us, length us, event | category | flops | bytes accessed | tf_op | source)
XLA Modules:
  0.0 882.9 jit_solution(13355797919147305140)
XLA Ops:
  12.7 6.9 all-to-all-start
  24.2 90.0 %all-to-all-done = f32[16,4,128,256]{2,3,1,0:T(8,128)} async-done(((f32[16,4,128,256]{2,3,1,0:T(8,128)}), f32[16,4,128,256]{2,3,1,0:T(8,128)}, u32[]{:S(2)}, u32[]{:S(2)}) %all-to-all-start) | async-done | bytes 8388640 | tf_op jit(solution)/shard_map/all_to_all | solution.py:64
  114.2 8.9 %copy.111 = f32[16,4,128,256]{3,2,0,1:T(8,128)} copy(f32[16,4,128,256]{2,3,1,0:T(8,128)} %all-to-all-done) | data formatting | bytes 16777216 | tf_op jit(solution)/shard_map/all_to_all | solution.py:64
  125.8 6.9 exponential_select_fusion.1
  136.8 7.0 fusion.33
  143.8 6.8 fusion.25
  159.2 578.2 %while.25 = (s32[]{:T(128)}, f32[256,5,128]{0,2,1:T(8,128)}, f32[256,5,128]{0,2,1:T(8,128)}, f32[256,5,128]{0,2,1:T(8,128)}, f32[256,5,128]{0,2,1:T(8,128)}, /*i...) while((s32[]{:T(128)}, f32[256,5,128]{0,2,1:T(8,128)}, ...), condition=%wide.region_3.4_spmd, body=%wide.region_1.3_spmd.sunk | while | flops 2526314752 | bytes 75933816 | solution.py:102
  171.4 5.9 collective-permute-done
  177.3 6.9 exponential_select_fusion.3
  184.1 35.3 %collective-permute-done.1 = f32[256,5,128]{0,2,1:T(8,128)S(1)} collective-permute-done((f32[256,5,128]{0,2,1:T(8,128)}, f32[256,5,128]{0,2,1:T(8,128)S(1)}, u32[]{:S(2)}, u32[]{:S(2)}) %collective-permute-start.1) | collective-permute-done | bytes 655392 | tf_op jit(solution)/shard_map/while/body/eval_jaxpr/ppermute | solution.py:10
  219.4 5.4 fusion.60
  260.2 6.9 exponential_select_fusion.3
  267.1 35.3 %collective-permute-done.1 = f32[256,5,128]{0,2,1:T(8,128)S(1)} collective-permute-done((f32[256,5,128]{0,2,1:T(8,128)}, f32[256,5,128]{0,2,1:T(8,128)S(1)}, u32[]{:S(2)}, u32[]{:S(2)}) %collective-permute-start.1) | collective-permute-done | bytes 655392 | tf_op jit(solution)/shard_map/while/body/eval_jaxpr/ppermute | solution.py:10
  338.2 6.1 collective-permute-done
  344.2 6.9 exponential_select_fusion.3
  351.1 35.3 %collective-permute-done.1 = f32[256,5,128]{0,2,1:T(8,128)S(1)} collective-permute-done((f32[256,5,128]{0,2,1:T(8,128)}, f32[256,5,128]{0,2,1:T(8,128)S(1)}, u32[]{:S(2)}, u32[]{:S(2)}) %collective-permute-start.1) | collective-permute-done | bytes 655392 | tf_op jit(solution)/shard_map/while/body/eval_jaxpr/ppermute | solution.py:10
  420.3 7.1 collective-permute-done
  427.4 6.9 exponential_select_fusion.3
  434.3 35.3 %collective-permute-done.1 = f32[256,5,128]{0,2,1:T(8,128)S(1)} collective-permute-done((f32[256,5,128]{0,2,1:T(8,128)}, f32[256,5,128]{0,2,1:T(8,128)S(1)}, u32[]{:S(2)}, u32[]{:S(2)}) %collective-permute-start.1) | collective-permute-done | bytes 655392 | tf_op jit(solution)/shard_map/while/body/eval_jaxpr/ppermute | solution.py:10
  502.3 7.4 collective-permute-done
  509.7 6.9 exponential_select_fusion.3
  516.6 35.3 %collective-permute-done.1 = f32[256,5,128]{0,2,1:T(8,128)S(1)} collective-permute-done((f32[256,5,128]{0,2,1:T(8,128)}, f32[256,5,128]{0,2,1:T(8,128)S(1)}, u32[]{:S(2)}, u32[]{:S(2)}) %collective-permute-start.1) | collective-permute-done | bytes 655392 | tf_op jit(solution)/shard_map/while/body/eval_jaxpr/ppermute | solution.py:10
  583.4 7.6 collective-permute-done
  591.0 6.9 exponential_select_fusion.3
  597.9 35.3 %collective-permute-done.1 = f32[256,5,128]{0,2,1:T(8,128)S(1)} collective-permute-done((f32[256,5,128]{0,2,1:T(8,128)}, f32[256,5,128]{0,2,1:T(8,128)S(1)}, u32[]{:S(2)}, u32[]{:S(2)}) %collective-permute-start.1) | collective-permute-done | bytes 655392 | tf_op jit(solution)/shard_map/while/body/eval_jaxpr/ppermute | solution.py:10
  663.7 7.8 collective-permute-done
  671.4 6.9 exponential_select_fusion.3
  678.3 35.3 %collective-permute-done.1 = f32[256,5,128]{0,2,1:T(8,128)S(1)} collective-permute-done((f32[256,5,128]{0,2,1:T(8,128)}, f32[256,5,128]{0,2,1:T(8,128)S(1)}, u32[]{:S(2)}, u32[]{:S(2)}) %collective-permute-start.1) | collective-permute-done | bytes 655392 | tf_op jit(solution)/shard_map/while/body/eval_jaxpr/ppermute | solution.py:10
  737.3 8.7 copy.131
  750.0 10.4 %collective-permute-done.4 = f32[256,5,128]{2,0,1:T(8,128)S(1)} collective-permute-done((f32[256,5,128]{2,0,1:T(8,128)S(1)}, f32[256,5,128]{2,0,1:T(8,128)S(1)}, u32[]{:S(2)}, u32[]{:S(2)}) %collective-permute-start.4) | collective-permute-done | bytes 655392 | tf_op jit(solution)/shard_map/ppermute | solution.py:10
  760.4 22.7 %collective-permute-done.5 = f32[256,5,128]{2,0,1:T(8,128)S(1)} collective-permute-done((f32[256,5,128]{2,0,1:T(8,128)S(1)}, f32[256,5,128]{2,0,1:T(8,128)S(1)}, u32[]{:S(2)}, u32[]{:S(2)}) %collective-permute-start.5) | collective-permute-done | bytes 655392 | tf_op jit(solution)/shard_map/ppermute | solution.py:10
  783.1 91.1 %reduce-scatter.2.cloned.1.call-done = f32[4,128,256]{2,1,0:T(8,128)} async-done(((f32[4,2048,256]{2,1,0:T(8,128)}), f32[4,128,256]{2,1,0:T(8,128)}) %reduce-scatter.2.cloned.1.call-update) | async-done | bytes 524304 | tf_op jit(solution)/shard_map/reduce_scatter | solution.py:111
  (227 shorter events, 266.2 us)
Async XLA Ops:
  12.7 101.5 %all-to-all-start = ((f32[16,4,128,256]{2,3,1,0:T(8,128)}), f32[16,4,128,256]{2,3,1,0:T(8,128)}, u32[]{:S(2)}, u32[]{:S(2)}) async-start(f32[16,4,128,256]{2,3,1,0:T(8,128)} %stack.2), calls=%async_computation | async-start | bytes 16777216 | tf_op jit(solution)/shard_map/all_to_all | solution.py:64
  19.6 854.6 %reduce-scatter.2.cloned.1.call-start = ((), (), s32[]{:S(2)}) async-start(), calls=%async_computation.2 | async-start | bytes 8912896 | tf_op jit(solution)/shard_map/reduce_scatter | solution.py:111
  160.2 17.1 %collective-permute-start = (f32[256,5,128]{0,2,1:T(8,128)}, f32[256,5,128]{0,2,1:T(8,128)S(1)}, u32[]{:S(2)}, u32[]{:S(2)}) collective-permute-start(f32[256,5,128]{0,2,1:T(8,128)} %get-tuple-element.556), channel_id=1, source_target_pairs={{0,1},{1,2},{2,3},{3,4},{4,5},{5,6},{6,7},{7,0},{8,9},{9,10},{10,1... | collective-permute-start | bytes 1966088 | tf_op jit(solution)/shard_map/while/body/eval_jaxpr/ppermute | solution.py:10
  161.5 74.4 %collective-permute-start.3 = (f32[256,5,128]{0,2,1:T(8,128)}, f32[256,5,128]{0,2,1:T(8,128)}, u32[]{:S(2)}, u32[]{:S(2)}) collective-permute-start(f32[256,5,128]{0,2,1:T(8,128)} %get-tuple-element.559), channel_id=1, source_target_pairs={{0,1},{1,2},{2,3},{3,4},{4,5},{5,6},{6,7},{7,0},{8,9},{9,10},{10,1... | collective-permute-start | bytes 1966088 | tf_op jit(solution)/shard_map/while/body/eval_jaxpr/ppermute | solution.py:10
  164.1 77.1 %collective-permute-start.2 = (f32[256,5,128]{0,2,1:T(8,128)}, f32[256,5,128]{0,2,1:T(8,128)}, u32[]{:S(2)}, u32[]{:S(2)}) collective-permute-start(f32[256,5,128]{0,2,1:T(8,128)} %get-tuple-element.558), channel_id=1, source_target_pairs={{0,1},{1,2},{2,3},{3,4},{4,5},{5,6},{6,7},{7,0},{8,9},{9,10},{10,1... | collective-permute-start | bytes 1966088 | tf_op jit(solution)/shard_map/while/body/eval_jaxpr/ppermute | solution.py:10
  165.4 54.0 %collective-permute-start.1 = (f32[256,5,128]{0,2,1:T(8,128)}, f32[256,5,128]{0,2,1:T(8,128)S(1)}, u32[]{:S(2)}, u32[]{:S(2)}) collective-permute-start(f32[256,5,128]{0,2,1:T(8,128)} %get-tuple-element.557), channel_id=1, source_target_pairs={{0,1},{1,2},{2,3},{3,4},{4,5},{5,6},{6,7},{7,0},{8,9},{9,10},{10,1... | collective-permute-start | bytes 1966088 | tf_op jit(solution)/shard_map/while/body/eval_jaxpr/ppermute | solution.py:10
  244.1 16.2 %collective-permute-start = (f32[256,5,128]{0,2,1:T(8,128)}, f32[256,5,128]{0,2,1:T(8,128)S(1)}, u32[]{:S(2)}, u32[]{:S(2)}) collective-permute-start(f32[256,5,128]{0,2,1:T(8,128)} %get-tuple-element.556), channel_id=1, source_target_pairs={{0,1},{1,2},{2,3},{3,4},{4,5},{5,6},{6,7},{7,0},{8,9},{9,10},{10,1... | collective-permute-start | bytes 1966088 | tf_op jit(solution)/shard_map/while/body/eval_jaxpr/ppermute | solution.py:10
  246.3 72.6 %collective-permute-start.3 = (f32[256,5,128]{0,2,1:T(8,128)}, f32[256,5,128]{0,2,1:T(8,128)}, u32[]{:S(2)}, u32[]{:S(2)}) collective-permute-start(f32[256,5,128]{0,2,1:T(8,128)} %get-tuple-element.559), channel_id=1, source_target_pairs={{0,1},{1,2},{2,3},{3,4},{4,5},{5,6},{6,7},{7,0},{8,9},{9,10},{10,1... | collective-permute-start | bytes 1966088 | tf_op jit(solution)/shard_map/while/body/eval_jaxpr/ppermute | solution.py:10
  248.0 76.2 %collective-permute-start.2 = (f32[256,5,128]{0,2,1:T(8,128)}, f32[256,5,128]{0,2,1:T(8,128)}, u32[]{:S(2)}, u32[]{:S(2)}) collective-permute-start(f32[256,5,128]{0,2,1:T(8,128)} %get-tuple-element.558), channel_id=1, source_target_pairs={{0,1},{1,2},{2,3},{3,4},{4,5},{5,6},{6,7},{7,0},{8,9},{9,10},{10,1... | collective-permute-start | bytes 1966088 | tf_op jit(solution)/shard_map/while/body/eval_jaxpr/ppermute | solution.py:10
  250.1 52.3 %collective-permute-start.1 = (f32[256,5,128]{0,2,1:T(8,128)}, f32[256,5,128]{0,2,1:T(8,128)S(1)}, u32[]{:S(2)}, u32[]{:S(2)}) collective-permute-start(f32[256,5,128]{0,2,1:T(8,128)} %get-tuple-element.557), channel_id=1, source_target_pairs={{0,1},{1,2},{2,3},{3,4},{4,5},{5,6},{6,7},{7,0},{8,9},{9,10},{10,1... | collective-permute-start | bytes 1966088 | tf_op jit(solution)/shard_map/while/body/eval_jaxpr/ppermute | solution.py:10
  327.0 17.2 %collective-permute-start = (f32[256,5,128]{0,2,1:T(8,128)}, f32[256,5,128]{0,2,1:T(8,128)S(1)}, u32[]{:S(2)}, u32[]{:S(2)}) collective-permute-start(f32[256,5,128]{0,2,1:T(8,128)} %get-tuple-element.556), channel_id=1, source_target_pairs={{0,1},{1,2},{2,3},{3,4},{4,5},{5,6},{6,7},{7,0},{8,9},{9,10},{10,1... | collective-permute-start | bytes 1966088 | tf_op jit(solution)/shard_map/while/body/eval_jaxpr/ppermute | solution.py:10
  330.1 72.8 %collective-permute-start.3 = (f32[256,5,128]{0,2,1:T(8,128)}, f32[256,5,128]{0,2,1:T(8,128)}, u32[]{:S(2)}, u32[]{:S(2)}) collective-permute-start(f32[256,5,128]{0,2,1:T(8,128)} %get-tuple-element.559), channel_id=1, source_target_pairs={{0,1},{1,2},{2,3},{3,4},{4,5},{5,6},{6,7},{7,0},{8,9},{9,10},{10,1... | collective-permute-start | bytes 1966088 | tf_op jit(solution)/shard_map/while/body/eval_jaxpr/ppermute | solution.py:10
  330.9 77.3 %collective-permute-start.2 = (f32[256,5,128]{0,2,1:T(8,128)}, f32[256,5,128]{0,2,1:T(8,128)}, u32[]{:S(2)}, u32[]{:S(2)}) collective-permute-start(f32[256,5,128]{0,2,1:T(8,128)} %get-tuple-element.558), channel_id=1, source_target_pairs={{0,1},{1,2},{2,3},{3,4},{4,5},{5,6},{6,7},{7,0},{8,9},{9,10},{10,1... | collective-permute-start | bytes 1966088 | tf_op jit(solution)/shard_map/while/body/eval_jaxpr/ppermute | solution.py:10
  333.9 52.5 %collective-permute-start.1 = (f32[256,5,128]{0,2,1:T(8,128)}, f32[256,5,128]{0,2,1:T(8,128)S(1)}, u32[]{:S(2)}, u32[]{:S(2)}) collective-permute-start(f32[256,5,128]{0,2,1:T(8,128)} %get-tuple-element.557), channel_id=1, source_target_pairs={{0,1},{1,2},{2,3},{3,4},{4,5},{5,6},{6,7},{7,0},{8,9},{9,10},{10,1... | collective-permute-start | bytes 1966088 | tf_op jit(solution)/shard_map/while/body/eval_jaxpr/ppermute | solution.py:10
  411.1 16.3 %collective-permute-start = (f32[256,5,128]{0,2,1:T(8,128)}, f32[256,5,128]{0,2,1:T(8,128)S(1)}, u32[]{:S(2)}, u32[]{:S(2)}) collective-permute-start(f32[256,5,128]{0,2,1:T(8,128)} %get-tuple-element.556), channel_id=1, source_target_pairs={{0,1},{1,2},{2,3},{3,4},{4,5},{5,6},{6,7},{7,0},{8,9},{9,10},{10,1... | collective-permute-start | bytes 1966088 | tf_op jit(solution)/shard_map/while/body/eval_jaxpr/ppermute | solution.py:10
  413.1 72.9 %collective-permute-start.3 = (f32[256,5,128]{0,2,1:T(8,128)}, f32[256,5,128]{0,2,1:T(8,128)}, u32[]{:S(2)}, u32[]{:S(2)}) collective-permute-start(f32[256,5,128]{0,2,1:T(8,128)} %get-tuple-element.559), channel_id=1, source_target_pairs={{0,1},{1,2},{2,3},{3,4},{4,5},{5,6},{6,7},{7,0},{8,9},{9,10},{10,1... | collective-permute-start | bytes 1966088 | tf_op jit(solution)/shard_map/while/body/eval_jaxpr/ppermute | solution.py:10
  413.1 78.2 %collective-permute-start.2 = (f32[256,5,128]{0,2,1:T(8,128)}, f32[256,5,128]{0,2,1:T(8,128)}, u32[]{:S(2)}, u32[]{:S(2)}) collective-permute-start(f32[256,5,128]{0,2,1:T(8,128)} %get-tuple-element.558), channel_id=1, source_target_pairs={{0,1},{1,2},{2,3},{3,4},{4,5},{5,6},{6,7},{7,0},{8,9},{9,10},{10,1... | collective-permute-start | bytes 1966088 | tf_op jit(solution)/shard_map/while/body/eval_jaxpr/ppermute | solution.py:10
  416.9 52.7 %collective-permute-start.1 = (f32[256,5,128]{0,2,1:T(8,128)}, f32[256,5,128]{0,2,1:T(8,128)S(1)}, u32[]{:S(2)}, u32[]{:S(2)}) collective-permute-start(f32[256,5,128]{0,2,1:T(8,128)} %get-tuple-element.557), channel_id=1, source_target_pairs={{0,1},{1,2},{2,3},{3,4},{4,5},{5,6},{6,7},{7,0},{8,9},{9,10},{10,1... | collective-permute-start | bytes 1966088 | tf_op jit(solution)/shard_map/while/body/eval_jaxpr/ppermute | solution.py:10
  494.2 15.5 %collective-permute-start = (f32[256,5,128]{0,2,1:T(8,128)}, f32[256,5,128]{0,2,1:T(8,128)S(1)}, u32[]{:S(2)}, u32[]{:S(2)}) collective-permute-start(f32[256,5,128]{0,2,1:T(8,128)} %get-tuple-element.556), channel_id=1, source_target_pairs={{0,1},{1,2},{2,3},{3,4},{4,5},{5,6},{6,7},{7,0},{8,9},{9,10},{10,1... | collective-permute-start | bytes 1966088 | tf_op jit(solution)/shard_map/while/body/eval_jaxpr/ppermute | solution.py:10
  495.2 73.2 %collective-permute-start.3 = (f32[256,5,128]{0,2,1:T(8,128)}, f32[256,5,128]{0,2,1:T(8,128)}, u32[]{:S(2)}, u32[]{:S(2)}) collective-permute-start(f32[256,5,128]{0,2,1:T(8,128)} %get-tuple-element.559), channel_id=1, source_target_pairs={{0,1},{1,2},{2,3},{3,4},{4,5},{5,6},{6,7},{7,0},{8,9},{9,10},{10,1... | collective-permute-start | bytes 1966088 | tf_op jit(solution)/shard_map/while/body/eval_jaxpr/ppermute | solution.py:10
  495.2 78.4 %collective-permute-start.2 = (f32[256,5,128]{0,2,1:T(8,128)}, f32[256,5,128]{0,2,1:T(8,128)}, u32[]{:S(2)}, u32[]{:S(2)}) collective-permute-start(f32[256,5,128]{0,2,1:T(8,128)} %get-tuple-element.558), channel_id=1, source_target_pairs={{0,1},{1,2},{2,3},{3,4},{4,5},{5,6},{6,7},{7,0},{8,9},{9,10},{10,1... | collective-permute-start | bytes 1966088 | tf_op jit(solution)/shard_map/while/body/eval_jaxpr/ppermute | solution.py:10
  498.9 53.0 %collective-permute-start.1 = (f32[256,5,128]{0,2,1:T(8,128)}, f32[256,5,128]{0,2,1:T(8,128)S(1)}, u32[]{:S(2)}, u32[]{:S(2)}) collective-permute-start(f32[256,5,128]{0,2,1:T(8,128)} %get-tuple-element.557), channel_id=1, source_target_pairs={{0,1},{1,2},{2,3},{3,4},{4,5},{5,6},{6,7},{7,0},{8,9},{9,10},{10,1... | collective-permute-start | bytes 1966088 | tf_op jit(solution)/shard_map/while/body/eval_jaxpr/ppermute | solution.py:10
  576.5 14.5 %collective-permute-start = (f32[256,5,128]{0,2,1:T(8,128)}, f32[256,5,128]{0,2,1:T(8,128)S(1)}, u32[]{:S(2)}, u32[]{:S(2)}) collective-permute-start(f32[256,5,128]{0,2,1:T(8,128)} %get-tuple-element.556), channel_id=1, source_target_pairs={{0,1},{1,2},{2,3},{3,4},{4,5},{5,6},{6,7},{7,0},{8,9},{9,10},{10,1... | collective-permute-start | bytes 1966088 | tf_op jit(solution)/shard_map/while/body/eval_jaxpr/ppermute | solution.py:10
  576.5 73.1 %collective-permute-start.3 = (f32[256,5,128]{0,2,1:T(8,128)}, f32[256,5,128]{0,2,1:T(8,128)}, u32[]{:S(2)}, u32[]{:S(2)}) collective-permute-start(f32[256,5,128]{0,2,1:T(8,128)} %get-tuple-element.559), channel_id=1, source_target_pairs={{0,1},{1,2},{2,3},{3,4},{4,5},{5,6},{6,7},{7,0},{8,9},{9,10},{10,1... | collective-permute-start | bytes 1966088 | tf_op jit(solution)/shard_map/while/body/eval_jaxpr/ppermute | solution.py:10
  576.5 78.4 %collective-permute-start.2 = (f32[256,5,128]{0,2,1:T(8,128)}, f32[256,5,128]{0,2,1:T(8,128)}, u32[]{:S(2)}, u32[]{:S(2)}) collective-permute-start(f32[256,5,128]{0,2,1:T(8,128)} %get-tuple-element.558), channel_id=1, source_target_pairs={{0,1},{1,2},{2,3},{3,4},{4,5},{5,6},{6,7},{7,0},{8,9},{9,10},{10,1... | collective-permute-start | bytes 1966088 | tf_op jit(solution)/shard_map/while/body/eval_jaxpr/ppermute | solution.py:10
  580.0 53.2 %collective-permute-start.1 = (f32[256,5,128]{0,2,1:T(8,128)}, f32[256,5,128]{0,2,1:T(8,128)S(1)}, u32[]{:S(2)}, u32[]{:S(2)}) collective-permute-start(f32[256,5,128]{0,2,1:T(8,128)} %get-tuple-element.557), channel_id=1, source_target_pairs={{0,1},{1,2},{2,3},{3,4},{4,5},{5,6},{6,7},{7,0},{8,9},{9,10},{10,1... | collective-permute-start | bytes 1966088 | tf_op jit(solution)/shard_map/while/body/eval_jaxpr/ppermute | solution.py:10
  657.8 13.6 %collective-permute-start = (f32[256,5,128]{0,2,1:T(8,128)}, f32[256,5,128]{0,2,1:T(8,128)S(1)}, u32[]{:S(2)}, u32[]{:S(2)}) collective-permute-start(f32[256,5,128]{0,2,1:T(8,128)} %get-tuple-element.556), channel_id=1, source_target_pairs={{0,1},{1,2},{2,3},{3,4},{4,5},{5,6},{6,7},{7,0},{8,9},{9,10},{10,1... | collective-permute-start | bytes 1966088 | tf_op jit(solution)/shard_map/while/body/eval_jaxpr/ppermute | solution.py:10
  657.8 72.2 %collective-permute-start.3 = (f32[256,5,128]{0,2,1:T(8,128)}, f32[256,5,128]{0,2,1:T(8,128)}, u32[]{:S(2)}, u32[]{:S(2)}) collective-permute-start(f32[256,5,128]{0,2,1:T(8,128)} %get-tuple-element.559), channel_id=1, source_target_pairs={{0,1},{1,2},{2,3},{3,4},{4,5},{5,6},{6,7},{7,0},{8,9},{9,10},{10,1... | collective-permute-start | bytes 1966088 | tf_op jit(solution)/shard_map/while/body/eval_jaxpr/ppermute | solution.py:10
  657.8 77.5 %collective-permute-start.2 = (f32[256,5,128]{0,2,1:T(8,128)}, f32[256,5,128]{0,2,1:T(8,128)}, u32[]{:S(2)}, u32[]{:S(2)}) collective-permute-start(f32[256,5,128]{0,2,1:T(8,128)} %get-tuple-element.558), channel_id=1, source_target_pairs={{0,1},{1,2},{2,3},{3,4},{4,5},{5,6},{6,7},{7,0},{8,9},{9,10},{10,1... | collective-permute-start | bytes 1966088 | tf_op jit(solution)/shard_map/while/body/eval_jaxpr/ppermute | solution.py:10
  660.2 53.3 %collective-permute-start.1 = (f32[256,5,128]{0,2,1:T(8,128)}, f32[256,5,128]{0,2,1:T(8,128)S(1)}, u32[]{:S(2)}, u32[]{:S(2)}) collective-permute-start(f32[256,5,128]{0,2,1:T(8,128)} %get-tuple-element.557), channel_id=1, source_target_pairs={{0,1},{1,2},{2,3},{3,4},{4,5},{5,6},{6,7},{7,0},{8,9},{9,10},{10,1... | collective-permute-start | bytes 1966088 | tf_op jit(solution)/shard_map/while/body/eval_jaxpr/ppermute | solution.py:10
  747.5 12.9 %collective-permute-start.4 = (f32[256,5,128]{2,0,1:T(8,128)S(1)}, f32[256,5,128]{2,0,1:T(8,128)S(1)}, u32[]{:S(2)}, u32[]{:S(2)}) collective-permute-start(f32[256,5,128]{2,0,1:T(8,128)S(1)} %copy.129), channel_id=1, source_target_pairs={{0,1},{1,2},{2,3},{3,4},{4,5},{5,6},{6,7},{7,0},{8,9},{9,10},{10,1... | collective-permute-start | bytes 1966088 | tf_op jit(solution)/shard_map/ppermute | solution.py:10
  748.9 34.3 %collective-permute-start.5 = (f32[256,5,128]{2,0,1:T(8,128)S(1)}, f32[256,5,128]{2,0,1:T(8,128)S(1)}, u32[]{:S(2)}, u32[]{:S(2)}) collective-permute-start(f32[256,5,128]{2,0,1:T(8,128)S(1)} %copy.130), channel_id=1, source_target_pairs={{0,1},{1,2},{2,3},{3,4},{4,5},{5,6},{6,7},{7,0},{8,9},{9,10},{10,1... | collective-permute-start | bytes 1966088 | tf_op jit(solution)/shard_map/ppermute | solution.py:10
  (35 other events, 200.6 us)
Sparse Core Ops, SparseCore 0:
  746.2 127.9 reduce-scatter.1
